TPU v7x, 32 devices: a whole 2x2x4 slice. The times are simulated.
32 devices in a mesh: grp: 2 (over x), pb: 8 (over z, y), ka: 2 (over core).
Axes of the slice: x: 2, y: 2, z: 4, core: 2. Of those that a mesh axis runs over, the one named last changes fastest.
Arguments:
- queries: bfloat16 [2048, 8192], P(('grp', 'pb', 'ka')), parts along dimension 0, may hold values from -2000 to 2000
- keys: bfloat16 [2048, 512], P(('grp', 'pb', 'ka')), parts along dimension 0, may hold values from -7 to 7
- values: bfloat16 [2048, 512], P(('grp', 'pb', 'ka')), parts along dimension 0, may hold values from -6 to 6
- panel_order: int32 [32], P('grp'), parts along dimension 0, may hold values from 0 to 15, as said below
- key_exp: int32 [32], P('grp'), parts along dimension 0, may hold values from -1 to 1
- value_exp: int32 [32], P('grp'), parts along dimension 0, may hold values from -1 to 1
Outputs:
- attended: bfloat16 [2048, 8192], P(('grp', 'pb', 'ka')), parts along dimension 0
There are 2 independent parts, one for each index of `grp`. A program takes and returns all parts, laid end to end along the dimension named above; each array names one. Nothing has to cross between parts.
Inputs may be any that keep to these rules, and one draw needn't show every extreme that they name: panel_order is a permutation of the panel numbers 0 to 15.
All inputs are finite; a program needn't handle non-finite values.
Results may differ from a plain program's by a relative error of at most 0.005.
Values may be sent and summed in bfloat16 or wider, within the bound.
A program may use at most 128 MiB of HBM per device.

v0:
```python
import jax
import jax.numpy as jnp
from jax import lax
from jax.sharding import PartitionSpec as P

HD = 128


NEG_BIG = -1e30
STEP_KEYS = 512


def panel_lookup(slot_ids, lookup_table):
    onehot = slot_ids[:, None] == jnp.arange(lookup_table.shape[0], dtype=jnp.int32)[None, :]
    return jnp.sum(jnp.where(onehot, lookup_table[None, :], 0), axis=1)


def absorb(carried, grouped, key_eff, value_eff, visible):
    accum, run_max, run_sum = carried
    scores = jnp.einsum(
        "qgeh,kgh->qgek", grouped, key_eff, preferred_element_type=jnp.float32
    ) * HD ** (-0.5)
    visible_mask = visible[:, None, None, :]
    scores = jnp.where(visible_mask, scores, NEG_BIG)
    new_max = jnp.maximum(run_max, jnp.max(scores, axis=-1))
    weights = jnp.where(visible_mask, jnp.exp(scores - new_max[..., None]), 0.0)
    rescale = jnp.exp(run_max - new_max)
    run_sum = run_sum * rescale + jnp.sum(weights, axis=-1)
    accum = accum * rescale[..., None] + jnp.einsum(
        "qgek,kgh->qgeh",
        weights.astype(jnp.bfloat16),
        value_eff,
        preferred_element_type=jnp.float32,
    )
    return (accum, new_max, run_sum)


def make_folder(grouped, query_pos, panel_len, slot_of, panel_order, key_exp, value_exp, kv_heads):

    def one_block(carried, key_rows, value_rows, first_row):
        key_count = key_rows.shape[0]
        rows_at = first_row + jnp.arange(key_count, dtype=jnp.int32)
        slot_ids = slot_of(rows_at // panel_len)
        key_scale = jnp.exp2(panel_lookup(slot_ids, key_exp).astype(jnp.float32)).astype(
            jnp.bfloat16
        )
        value_scale = jnp.exp2(panel_lookup(slot_ids, value_exp).astype(jnp.float32)).astype(
            jnp.bfloat16
        )
        key_eff = (key_rows * key_scale[:, None]).reshape(key_count, kv_heads, HD)
        value_eff = (value_rows * value_scale[:, None]).reshape(key_count, kv_heads, HD)
        key_pos = panel_lookup(slot_ids, panel_order) * panel_len + rows_at % panel_len
        visible = key_pos[None, :] <= query_pos[:, None]
        return absorb(carried, grouped, key_eff, value_eff, visible)

    def folder(carried, pieces, start_row):
        key_rows, value_rows = pieces
        key_count = key_rows.shape[0]
        panel_total = key_count // panel_len
        limit = max(STEP_KEYS, panel_len)
        per_step = max(
            (
                divisor
                for divisor in range(1, panel_total + 1)
                if panel_total % divisor == 0 and divisor * panel_len <= limit
            )
        )
        step_rows = per_step * panel_len
        blocks = key_count // step_rows
        key_blocks = key_rows.reshape(blocks, step_rows, key_rows.shape[1])
        value_blocks = value_rows.reshape(blocks, step_rows, value_rows.shape[1])

        def advance(running, block_item):
            key_block, value_block, block_index = block_item
            return (one_block(running, key_block, value_block, block_index * step_rows), None)

        carried, unused = lax.scan(
            advance, carried, (key_blocks, value_blocks, jnp.arange(blocks, dtype=jnp.int32))
        )
        return carried

    return folder


def fresh_state(rows_here, kv_heads, head_group):
    return (
        jnp.zeros((rows_here, kv_heads, head_group, HD), jnp.float32),
        jnp.full((rows_here, kv_heads, head_group), NEG_BIG, jnp.float32),
        jnp.zeros((rows_here, kv_heads, head_group), jnp.float32),
    )


def same_slot(position):
    return position


def local(queries, keys, values, panel_order, key_exp, value_exp):
    panel_len = keys.shape[0]
    head_group = queries.shape[1] // keys.shape[1]
    wide_size = lax.axis_size("pb")
    pair_size = lax.axis_size("ka")
    column = lax.axis_index("pb")
    own_rows = queries.shape[0]
    total_keys = panel_len * wide_size * pair_size
    total_queries = own_rows * wide_size * pair_size
    half_queries, half_keys, half_values = (
        lax.all_to_all(queries, "ka", split_axis=1, concat_axis=0, tiled=True),
        lax.all_to_all(keys, "ka", split_axis=1, concat_axis=0, tiled=True),
        lax.all_to_all(values, "ka", split_axis=1, concat_axis=0, tiled=True),
    )
    rows_here = half_queries.shape[0]
    local_heads = half_keys.shape[1] // HD
    query_pos = (
        total_keys - total_queries + column * rows_here + jnp.arange(rows_here, dtype=jnp.int32)
    )
    grouped = half_queries.reshape(rows_here, local_heads, head_group, HD)
    folder = make_folder(
        grouped, query_pos, panel_len, same_slot, panel_order, key_exp, value_exp, local_heads
    )
    accum, run_max, run_sum = folder(
        fresh_state(rows_here, local_heads, head_group),
        (
            lax.all_gather(half_keys, "pb", axis=0, tiled=True),
            lax.all_gather(half_values, "pb", axis=0, tiled=True),
        ),
        jnp.int32(0),
    )
    finished = (
        (accum / run_sum[..., None])
        .reshape(rows_here, local_heads * head_group * HD)
        .astype(jnp.bfloat16)
    )
    return lax.all_to_all(finished, "ka", split_axis=0, concat_axis=1, tiled=True)


def solution(mesh):
    placed = (
        P(("grp", "pb", "ka"), None),
        P(("grp", "pb", "ka"), None),
        P(("grp", "pb", "ka"), None),
        P("grp"),
        P("grp"),
        P("grp"),
    )
    return jax.shard_map(
        local, mesh=mesh, in_specs=placed, out_specs=P(("grp", "pb", "ka"), None), check_vma=False
    )
```

profile of v0, /device:TPU:1, one launch (start us, length us, event | category | flops | bytes accessed | tf_op | source)
XLA Modules:
  0.0 107.7 jit_solution(17507174625284312658)
XLA Ops:
  0.0 0.0 copy-start.4
  0.0 0.0 copy-start.3
  0.0 0.0 copy-start.2
  0.0 1.5 %copy.71 = bf16[8,2,8,256]{3,2,0,1:T(8,128)(2,1)} copy(bf16[8,2,8,256]{3,2,1,0:T(8,128)(2,1)} %bitcast.91) | data formatting | bytes 131072 | tf_op jit(solution)/shard_map/all_to_all | solution.py:109
  1.5 3.3 %all-to-all-start.2 = ((bf16[64,2,256]{2,0,1:T(8,128)(2,1)}), bf16[64,2,256]{2,0,1:T(8,128)(2,1)S(1)}, u32[]{:S(2)}, u32[]{:S(2)}) async-start(bf16[64,2,256]{2,0,1:T(8,128)(2,1)} %bitcast.59), calls=%async_computation.2 | async-start | bytes 131072 | tf_op jit(solution)/shard_map/all_to_all | solution.py:109
  4.9 1.5 %copy.72 = bf16[8,2,8,256]{3,2,0,1:T(8,128)(2,1)} copy(bf16[8,2,8,256]{3,2,1,0:T(8,128)(2,1)} %bitcast.92) | data formatting | bytes 131072 | tf_op jit(solution)/shard_map/all_to_all | solution.py:108
  6.3 0.0 all-to-all-done.2
  6.3 3.3 %all-to-all-start = ((bf16[64,2,256]{2,0,1:T(8,128)(2,1)}), bf16[64,2,256]{2,0,1:T(8,128)(2,1)S(1)}, u32[]{:S(2)}, u32[]{:S(2)}) async-start(bf16[64,2,256]{2,0,1:T(8,128)(2,1)} %bitcast.60), calls=%async_computation | async-start | bytes 131072 | tf_op jit(solution)/shard_map/all_to_all | solution.py:108
  9.7 27.1 %all_gather.7 = bf16[1024,256]{1,0:T(8,128)(2,1)S(1)} all-gather(bf16[128,256]{1,0:T(8,128)(2,1)S(1)} %bitcast.89), channel_id=1, replica_groups=mesh['grp'=2,'pb'=8,'ka'=2] {'pb'}, dimensions={0}, use_global_device_ids=true | all-gather | bytes 589824 | tf_op jit(solution)/shard_map/all_gather | solution.py:124
  36.8 2.3 %copy.70 = bf16[8,2,8,4096]{3,2,0,1:T(8,128)(2,1)} copy(bf16[8,2,8,4096]{3,2,1,0:T(8,128)(2,1)} %bitcast.88) | data formatting | bytes 2097152 | tf_op jit(solution)/shard_map/all_to_all | solution.py:107
  39.1 0.0 all-to-all-done
  39.1 9.6 %all-to-all-start.1 = ((bf16[64,2,4096]{2,0,1:T(8,128)(2,1)}), bf16[64,2,4096]{2,0,1:T(8,128)(2,1)S(1)}, u32[]{:S(2)}, u32[]{:S(2)}) async-start(bf16[64,2,4096]{2,0,1:T(8,128)(2,1)} %bitcast.58), calls=%async_computation.1 | async-start | bytes 2097152 | tf_op jit(solution)/shard_map/all_to_all | solution.py:107
  48.7 25.3 %all_gather.6 = bf16[1024,256]{1,0:T(8,128)(2,1)S(1)} all-gather(bf16[128,256]{1,0:T(8,128)(2,1)S(1)} %bitcast.90), channel_id=1, replica_groups=mesh['grp'=2,'pb'=8,'ka'=2] {'pb'}, dimensions={0}, use_global_device_ids=true | all-gather | bytes 589824 | tf_op jit(solution)/shard_map/all_gather | solution.py:123
  74.0 0.0 all-to-all-done.1
  74.0 0.2 copy.66
  74.3 0.4 copy.51
  74.7 0.0 copy-done.4
  74.7 0.0 copy-done.3
  74.7 0.0 copy-done.2
  74.7 18.5 %while.17 = (s32[]{:T(128)}, f32[128,2,16,128]{0,3,2,1:T(8,128)}, f32[128,2,16]{0,2,1:T(8,128)S(1)}, f32[128,2,16]{0,2,1:T(8,128)S(1)}, s32[2]{0:T(128)S(1)}, /*...) while((s32[]{:T(128)}, f32[128,2,16,128]{0,3,2,1:T(8,128)}, ...), condition=%wide.region_6.7_spmd.clone, body=%wide.region_0.6_spmd.clone.sunk | while | flops 1103786624 | bytes 50357692 | solution.py:77
  74.7 0.6 dynamic_slice.28
  75.9 0.1 select_reduce_fusion.4
  76.0 0.1 broadcast_compare_fusion.2
  76.2 0.1 copy.75
  76.4 0.1 copy.76
  76.5 0.0 copy-start
  76.5 1.4 %fusion.37 = (f32[128,2,16]{0,2,1:T(8,128)S(1)}, f32[2,512,128,16]{2,1,3,0:T(8,128)S(1)}) fusion(pred[128,512]{0,1:T(8,128)(4,1)S(1)} %broadcast_compare_fusion.2, bf16[128,2,16,128]{3,0,2,1:T(8,128)(2,1)S(1)} %get-tuple-element.430, bf16[512,2,128]{0,2,1:T(8,128)(2,1)S(1)} %bitcast.81, bf16[512]{0:T(512)(128)(2,1)S(1)} %get-tuple-element.385), kind=kOutput, calls=%fused_computation.3.clone.1 | convolution fusion | flops 543682560 | bytes 9782272 | tf_op jit(solution)/shard_map/while/body/eval_jaxpr/qgeh,kgh->qgek/dot_general | solution.py:20
  78.0 2.1 %fusion.38 = f32[128,2,16]{0,2,1:T(8,128)S(1)} fusion(f32[2,512,128,16]{2,1,3,0:T(8,128)S(1)} %get-tuple-element.386, f32[128,2,16]{0,2,1:T(8,128)S(1)} %select_maximum_fusion.2, pred[128,512]{0,1:T(8,128)(4,1)S(1)} %broadcast_compare_fusion.2), kind=kLoop, calls=%fused_computation.4.clone.1 | loop fusion | flops 10481664 | bytes 8486912 | tf_op jit(solution)/shard_map/while/body/eval_jaxpr/reduce_sum | solution.py:28
  80.1 0.0 copy-done
  80.1 2.6 %bitcast_add_fusion.2 = f32[128,2,16,128]{0,3,2,1:T(8,128)S(1)} fusion(f32[128,2,16,128]{0,3,2,1:T(8,128)S(1)} %copy-done, f32[2,512,128,16]{2,1,3,0:T(8,128)S(1)} %get-tuple-element.386, f32[128,2,16]{0,2,1:T(8,128)S(1)} %select_maximum_fusion.2, pred[128,512]{0,1:T(8,128)(4,1)S(1)} %broadcast_compare_fusion.2, ...), kind=kOutput, calls=%fused_computation.8.clone.1 | convolution fusion | flops 549453824 | bytes 12944385 | tf_op jit(solution)/shard_map/while/body/eval_jaxpr/qgek,kgh->qgeh/dot_general | solution.py:29
  82.6 0.0 copy-start.1
  82.7 1.3 %copy-done.1 = f32[128,2,16,128]{0,3,2,1:T(8,128)} copy-done((f32[128,2,16,128]{0,3,2,1:T(8,128)}, f32[128,2,16,128]{0,3,2,1:T(8,128)S(1)}, u32[]{:S(2)}) %copy-start.1) | copy-done | bytes 2097176 | tf_op jit(solution)/shard_map/while
  84.0 0.6 dynamic_slice.28
  85.1 0.1 select_reduce_fusion.4
  85.2 0.1 broadcast_compare_fusion.2
  85.4 0.1 copy.75
  85.6 0.1 copy.76
  85.7 0.0 copy-start
  85.7 1.4 %fusion.37 = (f32[128,2,16]{0,2,1:T(8,128)S(1)}, f32[2,512,128,16]{2,1,3,0:T(8,128)S(1)}) fusion(pred[128,512]{0,1:T(8,128)(4,1)S(1)} %broadcast_compare_fusion.2, bf16[128,2,16,128]{3,0,2,1:T(8,128)(2,1)S(1)} %get-tuple-element.430, bf16[512,2,128]{0,2,1:T(8,128)(2,1)S(1)} %bitcast.81, bf16[512]{0:T(512)(128)(2,1)S(1)} %get-tuple-element.385), kind=kOutput, calls=%fused_computation.3.clone.1 | convolution fusion | flops 543682560 | bytes 9782272 | tf_op jit(solution)/shard_map/while/body/eval_jaxpr/qgeh,kgh->qgek/dot_general | solution.py:20
  87.2 2.1 %fusion.38 = f32[128,2,16]{0,2,1:T(8,128)S(1)} fusion(f32[2,512,128,16]{2,1,3,0:T(8,128)S(1)} %get-tuple-element.386, f32[128,2,16]{0,2,1:T(8,128)S(1)} %select_maximum_fusion.2, pred[128,512]{0,1:T(8,128)(4,1)S(1)} %broadcast_compare_fusion.2), kind=kLoop, calls=%fused_computation.4.clone.1 | loop fusion | flops 10481664 | bytes 8486912 | tf_op jit(solution)/shard_map/while/body/eval_jaxpr/reduce_sum | solution.py:28
  89.3 0.0 copy-done
  89.3 2.6 %bitcast_add_fusion.2 = f32[128,2,16,128]{0,3,2,1:T(8,128)S(1)} fusion(f32[128,2,16,128]{0,3,2,1:T(8,128)S(1)} %copy-done, f32[2,512,128,16]{2,1,3,0:T(8,128)S(1)} %get-tuple-element.386, f32[128,2,16]{0,2,1:T(8,128)S(1)} %select_maximum_fusion.2, pred[128,512]{0,1:T(8,128)(4,1)S(1)} %broadcast_compare_fusion.2, ...), kind=kOutput, calls=%fused_computation.8.clone.1 | convolution fusion | flops 549453824 | bytes 12944385 | tf_op jit(solution)/shard_map/while/body/eval_jaxpr/qgek,kgh->qgeh/dot_general | solution.py:29
  91.9 0.0 copy-start.1
  91.9 1.3 %copy-done.1 = f32[128,2,16,128]{0,3,2,1:T(8,128)} copy-done((f32[128,2,16,128]{0,3,2,1:T(8,128)}, f32[128,2,16,128]{0,3,2,1:T(8,128)S(1)}, u32[]{:S(2)}) %copy-start.1) | copy-done | bytes 2097176 | tf_op jit(solution)/shard_map/while
  93.2 1.8 %divide_convert_fusion = bf16[128,2,16,128]{0,3,2,1:T(8,128)(2,1)S(1)} fusion(f32[128,2,16,128]{0,3,2,1:T(8,128)} %get-tuple-element.158, f32[128,2,16]{0,2,1:T(8,128)S(1)} %get-tuple-element.159), kind=kLoop, calls=%fused_computation.45 | loop fusion | flops 1048576 | bytes 3162112 | tf_op jit(solution)/shard_map/convert_element_type | solution.py:131
  95.1 1.0 copy.53
  96.0 0.5 convert_element_type.54
  96.5 10.1 %all_to_all.70 = bf16[2,64,4096]{2,1,0:T(8,128)(2,1)S(1)} all-to-all(bf16[2,64,4096]{2,1,0:T(8,128)(2,1)S(1)} %convert_element_type.54), channel_id=1, replica_groups=mesh['grp'=2,'pb'=8,'ka'=2] {'ka'}, dimensions={0} | all-to-all | bytes 2097152 | tf_op jit(solution)/shard_map/all_to_all | solution.py:133
  106.7 1.0 copy.65
  (20 shorter events, 0.2 us)
Async XLA Ops:
  0.0 74.7 %copy-start.4 = (s32[16]{0:T(128)S(1)}, s32[16]{0:T(128)}, u32[]{:S(2)}) copy-start(s32[16]{0:T(128)} %param.13) | copy-start | bytes 196
  0.0 74.7 %copy-start.3 = (s32[16]{0:T(128)S(1)}, s32[16]{0:T(128)}, u32[]{:S(2)}) copy-start(s32[16]{0:T(128)} %param.12) | copy-start | bytes 196
  0.0 74.7 %copy-start.2 = (s32[16]{0:T(128)S(1)}, s32[16]{0:T(128)}, u32[]{:S(2)}) copy-start(s32[16]{0:T(128)} %param.11) | copy-start | bytes 196
  1.5 4.8 %all-to-all-start.2 = ((bf16[64,2,256]{2,0,1:T(8,128)(2,1)}), bf16[64,2,256]{2,0,1:T(8,128)(2,1)S(1)}, u32[]{:S(2)}, u32[]{:S(2)}) async-start(bf16[64,2,256]{2,0,1:T(8,128)(2,1)} %bitcast.59), calls=%async_computation.2 | async-start | bytes 131072 | tf_op jit(solution)/shard_map/all_to_all | solution.py:109
  6.3 32.8 %all-to-all-start = ((bf16[64,2,256]{2,0,1:T(8,128)(2,1)}), bf16[64,2,256]{2,0,1:T(8,128)(2,1)S(1)}, u32[]{:S(2)}, u32[]{:S(2)}) async-start(bf16[64,2,256]{2,0,1:T(8,128)(2,1)} %bitcast.60), calls=%async_computation | async-start | bytes 131072 | tf_op jit(solution)/shard_map/all_to_all | solution.py:108
  39.1 34.9 %all-to-all-start.1 = ((bf16[64,2,4096]{2,0,1:T(8,128)(2,1)}), bf16[64,2,4096]{2,0,1:T(8,128)(2,1)S(1)}, u32[]{:S(2)}, u32[]{:S(2)}) async-start(bf16[64,2,4096]{2,0,1:T(8,128)(2,1)} %bitcast.58), calls=%async_computation.1 | async-start | bytes 2097152 | tf_op jit(solution)/shard_map/all_to_all | solution.py:107
  76.5 3.6 %copy-start = (f32[128,2,16,128]{0,3,2,1:T(8,128)S(1)}, f32[128,2,16,128]{0,3,2,1:T(8,128)}, u32[]{:S(2)}) copy-start(f32[128,2,16,128]{0,3,2,1:T(8,128)} %get-tuple-element.408) | copy-start | bytes 6291460 | tf_op jit(solution)/shard_map/while
  82.6 1.3 %copy-start.1 = (f32[128,2,16,128]{0,3,2,1:T(8,128)}, f32[128,2,16,128]{0,3,2,1:T(8,128)S(1)}, u32[]{:S(2)}) copy-start(f32[128,2,16,128]{0,3,2,1:T(8,128)S(1)} %bitcast_add_fusion.2) | copy-start | bytes 6291460 | tf_op jit(solution)/shard_map/while
  85.7 3.6 %copy-start = (f32[128,2,16,128]{0,3,2,1:T(8,128)S(1)}, f32[128,2,16,128]{0,3,2,1:T(8,128)}, u32[]{:S(2)}) copy-start(f32[128,2,16,128]{0,3,2,1:T(8,128)} %get-tuple-element.408) | copy-start | bytes 6291460 | tf_op jit(solution)/shard_map/while
  91.9 1.3 %copy-start.1 = (f32[128,2,16,128]{0,3,2,1:T(8,128)}, f32[128,2,16,128]{0,3,2,1:T(8,128)S(1)}, u32[]{:S(2)}) copy-start(f32[128,2,16,128]{0,3,2,1:T(8,128)S(1)} %bitcast_add_fusion.2) | copy-start | bytes 6291460 | tf_op jit(solution)/shard_map/while
where the time goes:
time: 109 us; the launch traced here: 108 us
  blocking collectives  62.6 us (57%)
  starting transfers between devices  16.3 us (15%)
  local copies, waits for them, and re-layouts  12.9 us (12%)
  matrix products  7.97 us (7%)
  other arithmetic  6.58 us (6%)
  loops' own time  1.37 us (1%)
    all_gather x1, blocking collectives, local(): lax.all_gather(half_values, 'pb', axis=0, tiled=True)  27.1 us
    all_gather x1, blocking collectives, local(): lax.all_gather(half_keys, 'pb', axis=0, tiled=True)  25.3 us
    all_to_all x1, blocking collectives, local(): lax.all_to_all(finished, 'ka', split_axis=0, concat_axis=1, tiled=True)  10.1 us
    all_to_all x1, starting transfers between devices, local(): lax.all_to_all(queries, 'ka', split_axis=1, concat_axis=0, tiled=True)  9.58 us
    dot_general x2, matrix products, absorb(): jnp.einsum('qgek,kgh->qgeh', weights.astype(jnp.bfloat16), value_eff, pre...  5.11 us
    reduce_sum x2, other arithmetic, absorb(): run_sum = run_sum * rescale + jnp.sum(weights, axis=-1)  4.13 us
    all_to_all x1, starting transfers between devices, local(): lax.all_to_all(values, 'ka', split_axis=1, concat_axis=0, tiled=True)  3.34 us
    all_to_all x1, starting transfers between devices, local(): lax.all_to_all(keys, 'ka', split_axis=1, concat_axis=0, tiled=True)  3.34 us
  transfers between devices with their start and end apart: 3, of which 0 were waited for; matrix products, arithmetic and copies ran while one was open for 3% of the time, Pallas kernels for 0%

commit v1 on v0

v1 whole, which is shorter than its diff:
```python
import functools
import math

import jax
import jax.numpy as jnp
from jax import lax
from jax.experimental import pallas as pl
from jax.experimental.pallas import tpu as pltpu
from jax.sharding import PartitionSpec as P

HD = 128
NEG_BIG = -1e30
MESH = pl.DeviceIdType.MESH
TILE_HEADS = 8


def kernel(
    wide, q_hbm, k_hbm, v_hbm, order, key_exp, value_exp, o_hbm,
    qv, kv, ov, acc, top, vaug, in_sem, out_sem, send_sem, recv_sem,
):
    rows = qv.shape[0]
    panel = k_hbm.shape[0]
    width = k_hbm.shape[1]
    groups = width // HD
    per_group = qv.shape[1] // width
    outer = wide // 2
    block = 4 * panel
    pb, ka = lax.axis_index("pb"), lax.axis_index("ka")
    z, y = pb // 2, pb % 2

    def slot(zz, yy, kk):
        return (zz * 2 + yy) * 2 + kk

    def at(s):
        return kv.at[pl.ds(pl.multiple_of(s * panel, panel), panel)]

    def remote(s, way, to_pb, to_ka):
        return pltpu.make_async_remote_copy(
            src_ref=at(s), dst_ref=at(s), send_sem=send_sem.at[s, way], recv_sem=recv_sem.at[s],
            device_id={"pb": to_pb, "ka": to_ka}, device_id_type=MESH,
        )

    def each_way(zz, act):
        s = slot(zz, y, ka)

        @pl.when((zz <= z) & (z + 1 < outer))
        def _():
            act(remote(s, 0, jnp.minimum(pb + 2, wide - 1), ka))

        @pl.when((zz >= z) & (z >= 1))
        def _():
            act(remote(s, 1, jnp.maximum(pb - 2, 0), ka))

        act(remote(s, 2, z * 2 + 1 - y, ka))
        act(remote(s, 3, pb, 1 - ka))

    def across(zz):
        return remote(slot(zz, 1 - y, ka), 3, pb, 1 - ka)

    def arrived(s):
        remote(s, 3, pb, 1 - ka).wait_recv()

    def start(copy):
        copy.start()

    mine = slot(z, y, ka)
    k_in = pltpu.make_async_copy(k_hbm, at(mine).at[:, pl.ds(0, width)], in_sem.at[0])
    v_in = pltpu.make_async_copy(v_hbm, at(mine).at[:, pl.ds(width, width)], in_sem.at[1])
    q_in = pltpu.make_async_copy(q_hbm, qv, in_sem.at[2])
    k_in.start()
    v_in.start()
    q_in.start()

    barrier = pltpu.get_barrier_semaphore()
    pl.semaphore_signal(barrier, inc=1, device_id={"pb": pb, "ka": 1 - ka}, device_id_type=MESH)
    pl.semaphore_signal(
        barrier, inc=1, device_id={"pb": z * 2 + 1 - y, "ka": ka}, device_id_type=MESH
    )

    @pl.when(z + 1 < outer)
    def _():
        pl.semaphore_signal(
            barrier, inc=1, device_id={"pb": jnp.minimum(pb + 2, wide - 1), "ka": ka},
            device_id_type=MESH,
        )

    @pl.when(z >= 1)
    def _():
        pl.semaphore_signal(
            barrier, inc=1, device_id={"pb": jnp.maximum(pb - 2, 0), "ka": ka}, device_id_type=MESH
        )

    inside = (z + 1 < outer).astype(jnp.int32) + (z >= 1).astype(jnp.int32)
    pl.semaphore_wait(barrier, 2 + inside)

    k_in.wait()
    v_in.wait()
    each_way(z, start)

    acc[...] = jnp.zeros_like(acc)
    top[...] = jnp.full_like(top, NEG_BIG)
    vaug[:, :, HD:] = jnp.ones((groups, block, HD), jnp.bfloat16)
    q_in.wait()

    total_keys = panel * wide * 2
    total_queries = rows * wide * 2
    first_query = total_keys - total_queries + mine * rows
    lane = lax.broadcasted_iota(jnp.int32, (rows, block), 1)
    query_pos = first_query + lax.broadcasted_iota(jnp.int32, (rows, block), 0)

    def by_panel(ref, b):
        got = jnp.full((rows, block), ref[b * 4], jnp.int32)
        for j in range(1, 4):
            got = jnp.where(lane >= j * panel, ref[b * 4 + j], got)
        return got

    def compute(b):
        key_pos = by_panel(order, b) * panel + lane % panel
        bias = jnp.where(key_pos <= query_pos, 0.0, NEG_BIG)
        scale = jnp.exp2(by_panel(key_exp, b)[:8].astype(jnp.float32))
        scale = scale.astype(jnp.bfloat16).astype(jnp.float32)[:1] * (HD**-0.5 * math.log2(math.e))
        first = pl.multiple_of(b * block, block)
        for j in range(4):
            value_scale = jnp.full((16, HD), value_exp[b * 4 + j], jnp.int32).astype(jnp.float32)
            value_scale = jnp.exp2(value_scale).astype(jnp.bfloat16)[:1]
            for g in range(groups):
                value_rows = kv[pl.ds(first + j * panel, panel), width + g * HD : width + (g + 1) * HD]
                vaug[g, j * panel : (j + 1) * panel, :HD] = value_rows * value_scale
        for g in range(groups):
            key_rows = kv[pl.ds(first, block), g * HD : (g + 1) * HD]
            for e in range(g * per_group, (g + 1) * per_group, TILE_HEADS):
                heads = range(e, e + TILE_HEADS)
                span = pl.ds(e * rows, TILE_HEADS * rows)
                q = jnp.concatenate([qv[:, h * HD : (h + 1) * HD] for h in heads], axis=0)
                s = lax.dot_general(
                    q, key_rows, (((1,), (1,)), ((), ())), preferred_element_type=jnp.float32
                )
                s = s.reshape(TILE_HEADS, rows, block) * scale[None] + bias[None]
                s = s.reshape(TILE_HEADS * rows, block)
                old = top[span]
                new = jnp.maximum(old, jnp.max(s, axis=1, keepdims=True))
                top[span] = new
                fade = jnp.exp2(old - new)
                weights = jnp.exp2(s - jnp.concatenate([new] * (block // HD), axis=1))
                mixed = jnp.dot(
                    weights.astype(jnp.bfloat16), vaug[g], preferred_element_type=jnp.float32
                )
                acc[span] = acc[span] * jnp.concatenate([fade, fade], axis=1) + mixed

    below = z < outer - 1 - z
    near = jnp.where(below, z, outer - 1 - z)

    def step(t, carry):
        d = t + 1

        @pl.when(z - d >= 0)
        def _():
            arrived(slot(jnp.maximum(z - d, 0), y, ka))
            each_way(jnp.maximum(z - d, 0), start)

        @pl.when(z + d < outer)
        def _():
            arrived(slot(jnp.minimum(z + d, outer - 1), y, ka))
            each_way(jnp.minimum(z + d, outer - 1), start)

        half = (t + 1) // 2
        both = jnp.where(t % 2 == 1, z + half, z - half)
        rest = jnp.where(below, z + (t - near), z - (t - near))
        b = jnp.where(t <= 2 * near, both, rest)
        arrived(slot(b, 1 - y, ka))
        across(b).start()
        arrived(slot(b, y, 1 - ka))
        arrived(slot(b, 1 - y, 1 - ka))
        compute(b)
        return carry

    lax.fori_loop(0, outer, step, 0)

    for g in range(groups):
        for e in range(g * per_group, (g + 1) * per_group):
            part = acc[pl.ds(e * rows, rows)]
            ov[:, e * HD : (e + 1) * HD] = (part[:, :HD] / part[:, HD:]).astype(jnp.bfloat16)
        columns = pl.ds(g * per_group * HD, per_group * HD)
        pltpu.make_async_copy(ov.at[:, columns], o_hbm.at[:, columns], out_sem.at[g]).start()

    def finish(zz, carry):
        each_way(zz, lambda copy: copy.wait_send())
        across(zz).wait_send()
        return carry

    lax.fori_loop(0, outer, finish, 0)
    for g in range(groups):
        columns = pl.ds(g * per_group * HD, per_group * HD)
        pltpu.make_async_copy(ov.at[:, columns], o_hbm.at[:, columns], out_sem.at[g]).wait()


def local(queries, keys, values, panel_order, key_exp, value_exp):
    rows, columns = queries.shape
    panel, width = keys.shape
    wide = lax.axis_size("pb")
    panels = wide * lax.axis_size("ka")
    heads = columns // HD
    groups = width // HD
    smem = pl.BlockSpec(memory_space=pltpu.SMEM)
    hbm = pl.BlockSpec(memory_space=pl.ANY)
    return pl.pallas_call(
        functools.partial(kernel, wide),
        out_shape=jax.ShapeDtypeStruct((rows, columns), jnp.bfloat16),
        in_specs=[hbm, hbm, hbm, smem, smem, smem],
        out_specs=hbm,
        scratch_shapes=[
            pltpu.VMEM((rows, columns), jnp.bfloat16),
            pltpu.VMEM((panels * panel, 2 * width), jnp.bfloat16),
            pltpu.VMEM((rows, columns), jnp.bfloat16),
            pltpu.VMEM((heads * rows, 2 * HD), jnp.float32),
            pltpu.VMEM((heads * rows, HD), jnp.float32),
            pltpu.VMEM((groups, 4 * panel, 2 * HD), jnp.bfloat16),
            pltpu.SemaphoreType.DMA((3,)),
            pltpu.SemaphoreType.DMA((groups,)),
            pltpu.SemaphoreType.DMA((panels, 4)),
            pltpu.SemaphoreType.DMA((panels,)),
        ],
        compiler_params=pltpu.CompilerParams(
            collective_id=0, has_side_effects=True, vmem_limit_bytes=56 * 1024 * 1024
        ),
        cost_estimate=pl.CostEstimate(
            flops=4 * rows * columns * panels * panel,
            bytes_accessed=4 * rows * columns + 4 * panel * width,
            transcendentals=rows * heads * panels * panel,
        ),
    )(queries, keys, values, panel_order, key_exp, value_exp)


def solution(mesh):
    placed = (
        P(("grp", "pb", "ka"), None),
        P(("grp", "pb", "ka"), None),
        P(("grp", "pb", "ka"), None),
        P("grp"),
        P("grp"),
        P("grp"),
    )
    return jax.shard_map(
        local, mesh=mesh, in_specs=placed, out_specs=P(("grp", "pb", "ka"), None), check_vma=False
    )
```

time: 109 us -> 28.6 us (0.26)
  blocking collectives: 62.6 us -> 0 us
  Pallas kernels: 0 us -> 26.1 us
  starting transfers between devices: 16.3 us -> 0 us
  local copies, waits for them, and re-layouts: 12.9 us -> 2.26 us
  matrix products: 7.97 us -> 0 us
  other arithmetic: 6.58 us -> 0 us
  loops' own time: 1.37 us -> 0 us
    all_gather x2 -> x0, blocking collectives: 52.4 us -> none  [the longest x1 27.1 us: local(): lax.all_gather(half_values, 'pb', axis=0, tiled=True)]
    pallas_call x0 -> x1, Pallas kernels: none -> 26.1 us  [local(): pl.pallas_call(functools.partial(kernel, wide), out_shape=jax.ShapeDtypeS...]
    all_to_all x3 -> x0, starting transfers between devices: 16.3 us -> none  [the longest x1 9.58 us: local(): lax.all_to_all(queries, 'ka', split_axis=1, concat_axis=0, tiled=True)]
    all_to_all x1 -> x0, blocking collectives: 10.1 us -> none  [local(): lax.all_to_all(finished, 'ka', split_axis=0, concat_axis=1, tiled=True)]
    dot_general x4 -> x0, matrix products: 7.97 us -> none  [the longest x2 5.11 us: absorb(): jnp.einsum('qgek,kgh->qgeh', weights.astype(jnp.bfloat16), value_eff, pre...]
    all_to_all x4 -> x0, local copies, waits for them, and re-layouts: 6.31 us -> none  [the longest x1 2.29 us: local(): lax.all_to_all(queries, 'ka', split_axis=1, concat_axis=0, tiled=True)]
    reduce_sum x4 -> x0, other arithmetic: 4.33 us -> none  [the longest x2 4.13 us: absorb(): run_sum = run_sum * rescale + jnp.sum(weights, axis=-1)]
    while x10 -> x0, local copies, waits for them, and re-layouts: 2.65 us -> none
  transfers between devices with their start and end apart: 3 -> 0, of which waited for: 0 -> 0; matrix products, arithmetic and copies ran while one was open for 3% -> 0% of each run, Pallas kernels for 0% -> 0%
where the time goes in v1:
time: 28.6 us; the launch traced here: 28.4 us
  Pallas kernels  26.1 us (91%)
  local copies, waits for them, and re-layouts  2.26 us (8%)
    pallas_call x1, Pallas kernels, local(): pl.pallas_call(functools.partial(kernel, wide), out_shape=jax.ShapeDtypeS...  26.1 us
    unnamed x1, local copies, waits for them, and re-layouts  2.26 us

profile of v1, /device:TPU:1, one launch (start us, length us, event | category | flops | bytes accessed | tf_op | source)
XLA Modules:
  0.0 28.4 jit_solution(12698408748254516550)
XLA Ops:
  0.0 26.1 %shard_map.64 = bf16[64,8192]{1,0:T(8,128)(2,1)} custom-call(bf16[64,8192]{1,0:T(8,128)(2,1)} %q_hbm.1, bf16[64,512]{1,0:T(8,128)(2,1)} %k_hbm.1, bf16[64,512]{1,0:T(8,128)(2,1)} %v_hbm.1, s32[16]{0:T(128)} %order.1, s32[16]{0:T(128)} %key_exp.1, s32[16]{0:T(128)} %value_exp.1), custom_call_target="tpu_custom_call" | custom-call | flops 2147483648 | bytes 2228224 | tf_op jit(solution)/shard_map/pallas_call | solution.py:206
  26.1 2.3 %copy.8 = bf16[64,8192]{1,0:T(8,128)(2,1)} copy(bf16[64,8192]{1,0:T(8,128)(2,1)} %shard_map.64) | data formatting | bytes 2097152

commit v2 on v1

v2 whole, which is shorter than its diff:
```python
import functools
import math

import jax
import jax.numpy as jnp
from jax import lax
from jax.experimental import pallas as pl
from jax.experimental.pallas import tpu as pltpu
from jax.sharding import PartitionSpec as P

HD = 128
NEG_BIG = -1e30
MESH = pl.DeviceIdType.MESH
TILE_HEADS = 8
PIECE = 16


def kernel(
    wide, q_hbm, k_hbm, v_hbm, order, key_exp, value_exp, o_hbm,
    qv, kv, ov, acc, top, vaug, hide, factor, in_sem, out_sem, send_sem, recv_sem,
):
    rows = qv.shape[0]
    panel = k_hbm.shape[0]
    width = k_hbm.shape[1]
    groups = width // HD
    per_group = qv.shape[1] // width
    outer = wide // 2
    block = 4 * panel
    pieces = panel // PIECE
    pb, ka = lax.axis_index("pb"), lax.axis_index("ka")
    z, y = pb // 2, pb % 2

    def slot(zz, yy, kk):
        return (zz * 2 + yy) * 2 + kk

    def at(s, p=None):
        if p is None:
            return kv.at[pl.ds(pl.multiple_of(s * panel, panel), panel)]
        return kv.at[pl.ds(pl.multiple_of(s * panel + p * PIECE, PIECE), PIECE)]

    def remote(s, p, way, to_pb, to_ka):
        land = 0 if way == 3 or p is None else p
        return pltpu.make_async_remote_copy(
            src_ref=at(s, p), dst_ref=at(s, p),
            send_sem=send_sem.at[s, way], recv_sem=recv_sem.at[s, land],
            device_id={"pb": to_pb, "ka": to_ka}, device_id_type=MESH,
        )

    def each_way(zz, p, act):
        s = slot(zz, y, ka)

        @pl.when((zz <= z) & (z + 1 < outer))
        def _():
            act(remote(s, p, 0, jnp.minimum(pb + 2, wide - 1), ka))

        @pl.when((zz >= z) & (z >= 1))
        def _():
            act(remote(s, p, 1, jnp.maximum(pb - 2, 0), ka))

        act(remote(s, p, 2, z * 2 + 1 - y, ka))
        act(remote(s, p, 3, pb, 1 - ka))

    def across(zz, p):
        return remote(slot(zz, 1 - y, ka), p, 3, pb, 1 - ka)

    def arrived(s, p):
        remote(s, p, 2, pb, 1 - ka).wait_recv()

    def start(copy):
        copy.start()

    mine = slot(z, y, ka)
    k_in = pltpu.make_async_copy(k_hbm, at(mine).at[:, pl.ds(0, width)], in_sem.at[0])
    v_in = pltpu.make_async_copy(v_hbm, at(mine).at[:, pl.ds(width, width)], in_sem.at[1])
    q_in = pltpu.make_async_copy(q_hbm, qv, in_sem.at[2])
    k_in.start()
    v_in.start()
    q_in.start()

    barrier = pltpu.get_barrier_semaphore()
    pl.semaphore_signal(barrier, inc=1, device_id={"pb": pb, "ka": 1 - ka}, device_id_type=MESH)
    pl.semaphore_signal(
        barrier, inc=1, device_id={"pb": z * 2 + 1 - y, "ka": ka}, device_id_type=MESH
    )

    @pl.when(z + 1 < outer)
    def _():
        pl.semaphore_signal(
            barrier, inc=1, device_id={"pb": jnp.minimum(pb + 2, wide - 1), "ka": ka},
            device_id_type=MESH,
        )

    @pl.when(z >= 1)
    def _():
        pl.semaphore_signal(
            barrier, inc=1, device_id={"pb": jnp.maximum(pb - 2, 0), "ka": ka}, device_id_type=MESH
        )

    inside = (z + 1 < outer).astype(jnp.int32) + (z >= 1).astype(jnp.int32)
    pl.semaphore_wait(barrier, 2 + inside)

    k_in.wait()
    v_in.wait()
    for p in range(pieces):
        each_way(z, p, start)

    acc[...] = jnp.zeros_like(acc)
    top[...] = jnp.full_like(top, NEG_BIG)
    vaug[:, :, HD:] = jnp.ones((groups, block, HD), jnp.bfloat16)
    q_in.wait()

    total_keys = panel * wide * 2
    total_queries = rows * wide * 2
    first_query = total_keys - total_queries + mine * rows
    lane = lax.broadcasted_iota(jnp.int32, (rows, block), 1)
    query_pos = first_query + lax.broadcasted_iota(jnp.int32, (rows, block), 0)

    def by_panel(ref, b):
        got = jnp.full((rows, block), ref[b * 4], jnp.int32)
        for j in range(1, 4):
            got = jnp.where(lane >= j * panel, ref[b * 4 + j], got)
        return got

    def prepare(b):
        key_pos = by_panel(order, b) * panel + lane % panel
        hide[...] = jnp.where(key_pos <= query_pos, 0.0, NEG_BIG)
        scale = jnp.exp2(by_panel(key_exp, b)[:8].astype(jnp.float32))
        scale = scale.astype(jnp.bfloat16).astype(jnp.float32)
        factor[...] = scale * (HD**-0.5 * math.log2(math.e))

    def compute(b, g):
        first = pl.multiple_of(b * block, block)
        for j in range(4):
            value_scale = jnp.full((16, HD), value_exp[b * 4 + j], jnp.int32).astype(jnp.float32)
            value_scale = jnp.exp2(value_scale).astype(jnp.bfloat16)[:1]
            value_rows = kv[pl.ds(first + j * panel, panel), width + g * HD : width + (g + 1) * HD]
            vaug[g, j * panel : (j + 1) * panel, :HD] = value_rows * value_scale
        key_rows = kv[pl.ds(first, block), g * HD : (g + 1) * HD]
        for e in range(g * per_group, (g + 1) * per_group, TILE_HEADS):
            heads = range(e, e + TILE_HEADS)
            span = pl.ds(e * rows, TILE_HEADS * rows)
            q = jnp.concatenate([qv[:, h * HD : (h + 1) * HD] for h in heads], axis=0)
            s = lax.dot_general(
                q, key_rows, (((1,), (1,)), ((), ())), preferred_element_type=jnp.float32
            )
            s = s.reshape(TILE_HEADS, rows, block) * factor[:1][None] + hide[...][None]
            s = s.reshape(TILE_HEADS * rows, block)
            old = top[span]
            new = jnp.maximum(old, jnp.max(s, axis=1, keepdims=True))
            top[span] = new
            fade = jnp.exp2(old - new)
            weights = jnp.exp2(s - jnp.concatenate([new] * (block // HD), axis=1))
            mixed = jnp.dot(
                weights.astype(jnp.bfloat16), vaug[g], preferred_element_type=jnp.float32
            )
            acc[span] = acc[span] * jnp.concatenate([fade, fade], axis=1) + mixed

    def out_copy(g):
        columns = pl.ds(g * per_group * HD, per_group * HD)
        return pltpu.make_async_copy(ov.at[:, columns], o_hbm.at[:, columns], out_sem.at[g])

    def conclude(g):
        for e in range(g * per_group, (g + 1) * per_group):
            part = acc[pl.ds(e * rows, rows)]
            ov[:, e * HD : (e + 1) * HD] = (part[:, :HD] / part[:, HD:]).astype(jnp.bfloat16)
        out_copy(g).start()

    below = z < outer - 1 - z
    near = jnp.where(below, z, outer - 1 - z)

    def nth(t):
        half = (t + 1) // 2
        both = jnp.where(t % 2 == 1, z + half, z - half)
        rest = jnp.where(below, z + (t - near), z - (t - near))
        return jnp.clip(jnp.where(t <= 2 * near, both, rest), 0, outer - 1)

    def step(u, carry, last=False):
        d = u + 1
        b = nth(u)
        for p in range(pieces):

            @pl.when(z - d >= 0)
            def _():
                zz = jnp.maximum(z - d, 0)
                arrived(slot(zz, y, ka), p)
                each_way(zz, p, start)

            @pl.when(z + d < outer)
            def _():
                zz = jnp.minimum(z + d, outer - 1)
                arrived(slot(zz, y, ka), p)
                each_way(zz, p, start)

        for p in range(pieces):
            arrived(slot(b, 1 - y, ka), p)
            across(b, p).start()
        prepare(b)
        arrived(slot(b, y, 1 - ka), None)
        arrived(slot(b, 1 - y, 1 - ka), None)
        for g in range(groups):
            compute(b, g)
            if last:
                conclude(g)
        return carry

    lax.fori_loop(0, outer - 1, step, 0)
    step(outer - 1, 0, last=True)

    def finish(zz, carry):
        each_way(zz, None, lambda copy: copy.wait_send())
        across(zz, None).wait_send()
        return carry

    lax.fori_loop(0, outer, finish, 0)
    for g in range(groups):
        out_copy(g).wait()


def local(queries, keys, values, panel_order, key_exp, value_exp):
    rows, columns = queries.shape
    panel, width = keys.shape
    wide = lax.axis_size("pb")
    panels = wide * lax.axis_size("ka")
    heads = columns // HD
    groups = width // HD
    smem = pl.BlockSpec(memory_space=pltpu.SMEM)
    hbm = pl.BlockSpec(memory_space=pl.ANY)
    return pl.pallas_call(
        functools.partial(kernel, wide),
        out_shape=jax.ShapeDtypeStruct((rows, columns), jnp.bfloat16),
        in_specs=[hbm, hbm, hbm, smem, smem, smem],
        out_specs=hbm,
        scratch_shapes=[
            pltpu.VMEM((rows, columns), jnp.bfloat16),
            pltpu.VMEM((panels * panel, 2 * width), jnp.bfloat16),
            pltpu.VMEM((rows, columns), jnp.bfloat16),
            pltpu.VMEM((heads * rows, 2 * HD), jnp.float32),
            pltpu.VMEM((heads * rows, HD), jnp.float32),
            pltpu.VMEM((groups, 4 * panel, 2 * HD), jnp.bfloat16),
            pltpu.VMEM((rows, 4 * panel), jnp.float32),
            pltpu.VMEM((8, 4 * panel), jnp.float32),
            pltpu.SemaphoreType.DMA((3,)),
            pltpu.SemaphoreType.DMA((groups,)),
            pltpu.SemaphoreType.DMA((panels, 4)),
            pltpu.SemaphoreType.DMA((panels, panel // PIECE)),
        ],
        compiler_params=pltpu.CompilerParams(
            collective_id=0, has_side_effects=True, vmem_limit_bytes=56 * 1024 * 1024
        ),
        cost_estimate=pl.CostEstimate(
            flops=4 * rows * columns * panels * panel,
            bytes_accessed=4 * rows * columns + 4 * panel * width,
            transcendentals=rows * heads * panels * panel,
        ),
    )(queries, keys, values, panel_order, key_exp, value_exp)


def solution(mesh):
    placed = (
        P(("grp", "pb", "ka"), None),
        P(("grp", "pb", "ka"), None),
        P(("grp", "pb", "ka"), None),
        P("grp"),
        P("grp"),
        P("grp"),
    )
    return jax.shard_map(
        local, mesh=mesh, in_specs=placed, out_specs=P(("grp", "pb", "ka"), None), check_vma=False
    )
```

time: 28.6 us -> 27.3 us (0.955)
  Pallas kernels: 26.1 us -> 24.7 us
    pallas_call x1, Pallas kernels: 26.1 us -> 24.7 us  [local(): pl.pallas_call(functools.partial(kernel, wide), out_shape=jax.ShapeDtypeS...]
where the time goes in v2:
time: 27.3 us; the launch traced here: 27 us
  Pallas kernels  24.7 us (90%)
  local copies, waits for them, and re-layouts  2.26 us (8%)
    pallas_call x1, Pallas kernels, local(): pl.pallas_call(functools.partial(kernel, wide), out_shape=jax.ShapeDtypeS...  24.7 us
    unnamed x1, local copies, waits for them, and re-layouts  2.26 us

profile of v2, /device:TPU:1, one launch (start us, length us, event | category | flops | bytes accessed | tf_op | source)
XLA Modules:
  0.0 27.0 jit_solution(6749209323106286618)
XLA Ops:
  0.0 24.7 %shard_map.64 = bf16[64,8192]{1,0:T(8,128)(2,1)} custom-call(bf16[64,8192]{1,0:T(8,128)(2,1)} %q_hbm.1, bf16[64,512]{1,0:T(8,128)(2,1)} %k_hbm.1, bf16[64,512]{1,0:T(8,128)(2,1)} %v_hbm.1, s32[16]{0:T(128)} %order.1, s32[16]{0:T(128)} %key_exp.1, s32[16]{0:T(128)} %value_exp.1), custom_call_target="tpu_custom_call" | custom-call | flops 2147483648 | bytes 2228224 | tf_op jit(solution)/shard_map/pallas_call | solution.py:228
  24.7 2.3 %copy.8 = bf16[64,8192]{1,0:T(8,128)(2,1)} copy(bf16[64,8192]{1,0:T(8,128)(2,1)} %shard_map.64) | data formatting | bytes 2097152
